TPU v7x, 128 devices: a whole 4x4x4 slice. The times are simulated.
128 devices in a mesh: frame: 16 (over z_lo, y, core), space: 8 (over x, z_hi).
Axes of the slice: x: 4, y: 4, z: 4 (z_hi: 2, z_lo: 2; z = z_hi * 2 + z_lo), core: 2. Of those that a mesh axis runs over, the one named last changes fastest.
Arguments:
- q_spatial: bfloat16 [2, 16, 1536, 1152], P(None, 'frame', 'space'), may hold values from -220 to 220, as said below
- k_spatial: bfloat16 [2, 16, 1536, 1152], P(None, 'frame', 'space'), may hold values from -7 to 7, as said below
- v_spatial: bfloat16 [2, 16, 1536, 1152], P(None, 'frame', 'space'), may hold values from -6 to 6
- q_temporal: bfloat16 [2, 16, 1536, 1152], P(None, 'frame', 'space'), may hold values from -220 to 220, as said below
- k_temporal: bfloat16 [2, 16, 1536, 1152], P(None, 'frame', 'space'), may hold values from -7 to 7, as said below
- v_temporal: bfloat16 [2, 16, 1536, 1152], P(None, 'frame', 'space'), may hold values from -6 to 6
- grad_out: bfloat16 [2, 16, 1536, 1152], P(None, 'frame', 'space'), may hold values from -6 to 6
- inpaint_mask: int32 [2, 16, 1536], P(None, 'frame', 'space'), may hold values 0 or 1
- frame_order: int32 [16], replicated, may hold values from 0 to 15, each once
- rel_bias: float32 [16, 31], replicated, may hold values from -2 to 2
- w_qkv: bfloat16 [1152, 3456], replicated, may hold values from -0.1875 to 0.1875
- w_out: bfloat16 [1152, 1152], replicated, may hold values from -0.1875 to 0.1875
Outputs:
- grad_q_spatial: bfloat16 [2, 16, 1536, 1152], P(None, 'frame', 'space')
- grad_k_spatial: bfloat16 [2, 16, 1536, 1152], P(None, 'frame', 'space')
- grad_v_spatial: bfloat16 [2, 16, 1536, 1152], P(None, 'frame', 'space')
- grad_mid: bfloat16 [2, 16, 1536, 1152], P(None, 'frame', 'space')
Inputs may be any that keep to these rules, and one draw needn't show every extreme that they name: `q_spatial`: bfloat16 values. `k_spatial`: bfloat16 values. `q_temporal`: bfloat16 values. `k_temporal`: bfloat16 values. `frame_order`: each time position once.
All inputs are finite; a program needn't handle non-finite values. No bound on the sum of `inpaint_mask` on one device may be relied on, other than what follows from the above.
Results may differ from a plain program's by a relative error of at most 0.012.
Values may be sent and summed in bfloat16 or wider, within the bound.
A program may use at most 256 MiB of HBM per device.

v0:
```python
import functools

import jax
import jax.numpy as jnp
from jax import lax
from jax.experimental import pallas as pl
from jax.experimental.pallas import tpu as pltpu
from jax.sharding import PartitionSpec as P

HEADS = 16
E = 72
D = 1152
CLIPS = 2
FRAMES = 16
TOKENS = 192
SEQ = 1536
SPACE = 8
GROUPS = 3
ROWS = 128
BLOCK = 512
SCALE = E ** (-0.5)
LOG2E = 1.4426950408889634
MESH = pl.DeviceIdType.MESH
NN = (((1,), (0,)), ((), ()))
NT = (((1,), (1,)), ((), ()))
F32 = jnp.float32
BF16 = jnp.bfloat16


def dot(a, b, dims=NN):
    return lax.dot_general(a, b, dims, preferred_element_type=F32)


def softmax_grads(scores, dprob):
    weights = jnp.exp2(scores - jnp.max(scores, axis=1, keepdims=True))
    probs = weights * (1.0 / jnp.sum(weights, axis=1, keepdims=True))
    probs_low = probs.astype(BF16)
    delta = jnp.sum(probs_low.astype(F32) * dprob, axis=1, keepdims=True)
    return probs_low, (probs * ((dprob - delta) * SCALE)).astype(BF16)


def halves(low, high):
    lane = lax.broadcasted_iota(jnp.int32, low.shape, 1)
    return jnp.where(lane < 64, low, high)


def store_slabs(dst, main0, main1, third):
    for clip, main in enumerate((main0, main1)):
        by_head = main.reshape(SPACE, 2, E, 128)
        dst[:, clip, 0] = by_head[:, 0].astype(BF16)
        dst[:, clip, 1] = by_head[:, 1].astype(BF16)
    by_head = third.reshape(SPACE, 2, E, 128)
    even = by_head[:, 0].reshape(SPACE * E, 128)
    odd = by_head[:, 1].reshape(SPACE * E, 128)
    dst[:, 0, 2] = halves(even, pltpu.roll(odd, 64, 1)).reshape(SPACE, E, 128).astype(BF16)
    dst[:, 1, 2] = halves(pltpu.roll(even, 64, 1), odd).reshape(SPACE, E, 128).astype(BF16)


def temporal_kernel(
    qt, kt, vt, go, mask, fo_col, fo_row, rel_bias, qs, ks, vs, wqkv, wout,
    gm, recv,
    cot, tin, xg, bias, joined, gm_send, sin, send, wq, wo,
    t_send_sem, t_recv_sem, g_send_sem, g_recv_sem, s_send_sem, s_recv_sem, local_sem,
):
    mf, ms = lax.axis_index("frame"), lax.axis_index("space")
    loads = [
        pltpu.make_async_copy(src, dst, local_sem.at[n])
        for n, (src, dst) in enumerate(
            ((qs, sin.at[0]), (ks, sin.at[1]), (vs, sin.at[2]), (wqkv, wq), (wout, wo))
        )
    ]
    for copy in loads:
        copy.start()

    barrier = pltpu.get_barrier_semaphore()

    @pl.loop(1, FRAMES)
    def _(i):
        pl.semaphore_signal(barrier, inc=1, device_id=(lax.rem(mf + i, FRAMES), ms), device_id_type=MESH)

    @pl.loop(1, SPACE)
    def _(i):
        pl.semaphore_signal(barrier, inc=1, device_id=(mf, lax.rem(ms + i, SPACE)), device_id_type=MESH)

    pl.semaphore_wait(barrier, FRAMES + SPACE - 2)

    sources = (qt, kt, cot, vt)

    def t_copy(a, i):
        peer = lax.rem(mf + i, FRAMES)
        return pltpu.make_async_remote_copy(
            src_ref=sources[a].at[peer], dst_ref=tin.at[a, mf],
            send_sem=t_send_sem.at[a, i], recv_sem=t_recv_sem.at[a, i],
            device_id=(peer, ms), device_id_type=MESH,
        )

    def g_copy(i):
        peer = lax.rem(mf + i, FRAMES)
        return pltpu.make_async_remote_copy(
            src_ref=gm_send.at[peer], dst_ref=gm.at[mf],
            send_sem=g_send_sem.at[i], recv_sem=g_recv_sem.at[i],
            device_id=(peer, ms), device_id_type=MESH,
        )

    def s_copy(a, i):
        peer = lax.rem(ms + i, SPACE)
        return pltpu.make_async_remote_copy(
            src_ref=send.at[a, peer], dst_ref=recv.at[a, ms],
            send_sem=s_send_sem.at[a, i], recv_sem=s_recv_sem.at[a, i],
            device_id=(mf, peer), device_id_type=MESH,
        )

    def t_start(a):
        @pl.loop(1, FRAMES)
        def _(i):
            t_copy(a, i).start()

    t_start(0)
    t_start(1)
    cot[...] = (go[...].astype(F32) * mask[...].astype(F32)).astype(BF16)
    t_start(2)
    t_start(3)
    own = [
        pltpu.make_async_copy(sources[a].at[mf], tin.at[a, mf], local_sem.at[5 + a]) for a in range(4)
    ]
    for copy in own:
        copy.start()

    for a in range(3):
        loads[a].wait()

    @pl.loop(0, 3)
    def _(a):
        x = sin.at[a]
        main0 = x[0, 0:128, :].astype(F32).T
        main1 = x[1, 0:128, :].astype(F32).T
        third = jnp.concatenate([x[0, 128:192, :].astype(F32), x[1, 128:192, :].astype(F32)], axis=0).T
        store_slabs(send.at[a], main0, main1, third)
        for i in (2, 4, 6):
            s_copy(a, i).start()

    row = lax.broadcasted_iota(jnp.int32, (ROWS, ROWS), 0)
    col = lax.broadcasted_iota(jnp.int32, (ROWS, ROWS), 1)
    offset = jnp.where((row & 7) == (col & 7), fo_col[...] - fo_row[...] + (FRAMES - 1), -1)

    @pl.loop(0, HEADS)
    def _(h):
        total = jnp.full((ROWS, ROWS), -1e30, F32)
        for o in range(2 * FRAMES - 1):
            total = jnp.where(offset == o, rel_bias[h, o] * LOG2E, total)
        bias[h] = total

    for a in range(4):
        own[a].wait()

        @pl.loop(1, FRAMES)
        def _(i):
            t_copy(a, i).wait()

    @pl.loop(0, 3)
    def _(a):
        for i in (1, 7, 3, 5):
            s_copy(a, i).start()

    lane = lax.broadcasted_iota(jnp.int32, (1, 256), 1)

    @pl.loop(0, GROUPS)
    def _(g):
        for a in range(4):
            xg[a] = tin[a, :, g].astype(F32).reshape(ROWS, D).astype(BF16)
        carry = None
        for p in range(SPACE):
            window = slice(128 * p, 128 * p + 256)
            first = 16 * p
            m0 = jnp.where((lane >= first) & (lane < first + E), 1.0, 0.0).astype(BF16)
            m1 = jnp.where((lane >= first + E) & (lane < first + 2 * E), 1.0, 0.0).astype(BF16)

            def stacked(x):
                return jnp.concatenate([x * m0, x * m1], axis=0)

            q, k, c, v = (xg[a, :, window] for a in range(4))
            k2 = stacked(k)
            scores = dot(q, k2, NT)
            dprob = dot(c, stacked(v), NT)
            low, ds, low_t, ds_t = [], [], [], []
            for n in range(2):
                part = slice(128 * n, 128 * n + 128)
                pb, d = softmax_grads(scores[:, part] * (SCALE * LOG2E) + bias[2 * p + n], dprob[:, part])
                ds.append(d)
                low_t.append(pb.astype(F32).T.astype(BF16))
                ds_t.append(d.astype(F32).T.astype(BF16))
            outs = (
                dot(jnp.concatenate(ds, axis=1), k2),
                dot(jnp.concatenate(ds_t, axis=1), stacked(q)),
                dot(jnp.concatenate(low_t, axis=1), stacked(c)),
            )
            rows = pl.ds(pl.multiple_of(g * ROWS, ROWS), ROWS)
            for n, out in enumerate(outs):
                left = out[:, :128] if carry is None else out[:, :128] + carry[n]
                joined[rows, D * n + 128 * p:D * n + 128 * p + 128] = left.astype(BF16)
                if p == SPACE - 1:
                    joined[rows, D * n + 1024:D * n + D] = out[:, 128:].astype(BF16)
            carry = [out[:, 128:] for out in outs]

    loads[3].wait()
    mid = dot(joined[...], wq[...], NT)
    for g in range(GROUPS):
        gm_send[:, g] = mid[g * ROWS:(g + 1) * ROWS].reshape(FRAMES, 8, D).astype(BF16)

    @pl.loop(1, FRAMES)
    def _(i):
        g_copy(i).start()

    own_gm = pltpu.make_async_copy(gm_send.at[mf], gm.at[mf], local_sem.at[9])
    own_gm.start()
    own_gm.wait()

    @pl.loop(1, FRAMES)
    def _(i):
        g_copy(i).wait()

    loads[4].wait()
    mid = gm[...].astype(F32).reshape(CLIPS, TOKENS, D)
    mid = jnp.concatenate([mid[0, :128], mid[1, :128], mid[0, 128:], mid[1, 128:]], axis=0).astype(BF16)
    cot_t = dot(wo[...], mid, NT)
    store_slabs(send.at[3], cot_t[:, :128], cot_t[:, 128:256], cot_t[:, 256:])
    for i in (1, 7, 3, 5, 2, 4, 6):
        s_copy(3, i).start()
    own_s = [
        pltpu.make_async_copy(send.at[a, ms], recv.at[a, ms], local_sem.at[10 + a]) for a in range(4)
    ]
    for copy in own_s:
        copy.start()
    for copy in own_s:
        copy.wait()

    @pl.loop(0, 4)
    def _(a):
        @pl.loop(1, SPACE)
        def _(i):
            s_copy(a, i).wait()


def spatial_kernel(
    x, gq, gk, gv, q_t, k_t, v_t, c_t, q_n, c_n, sum_k, sum_v, thirds, send, recv,
    send_sem, recv_sem, local_sem,
):
    mf, ms = lax.axis_index("frame"), lax.axis_index("space")
    barrier = pltpu.get_barrier_semaphore()

    @pl.loop(1, SPACE)
    def _(i):
        pl.semaphore_signal(barrier, inc=1, device_id=(mf, lax.rem(ms + i, SPACE)), device_id_type=MESH)

    pl.semaphore_wait(barrier, SPACE - 1)

    def copy_of(a, i, clip, slab):
        peer = lax.rem(ms + i, SPACE)
        return pltpu.make_async_remote_copy(
            src_ref=send.at[a, peer, clip, slab], dst_ref=recv.at[a, ms, clip, slab],
            send_sem=send_sem.at[a, i, clip, slab], recv_sem=recv_sem.at[a, i, clip, slab],
            device_id=(mf, peer), device_id_type=MESH,
        )

    def start_slab(a, clip, slab):
        for i in (1, 7, 3, 5, 2, 4, 6):
            copy_of(a, i, clip, slab).start()

    def gather(a, clip, head, dst):
        for s in range(SPACE):
            dst[:, 128 * s:128 * s + 128] = x[a, s, clip, head]
        for m in range(SPACE // 2):
            low = x[a, 2 * m, clip, 2].astype(F32)
            high = x[a, 2 * m + 1, clip, 2].astype(F32)
            if head == 0:
                high = pltpu.roll(high, 64, 1)
            else:
                low = pltpu.roll(low, 64, 1)
            dst[:, 1024 + 128 * m:1152 + 128 * m] = halves(low, high).astype(BF16)

    def scatter(a, clip, head, tile, value):
        if tile < SPACE:
            send[a, tile, clip, head] = value.astype(BF16)
        elif head == 0:
            thirds[a, tile - SPACE] = value
        else:
            m = tile - SPACE
            other = thirds[a, m]
            send[a, 2 * m, clip, 2] = halves(other, pltpu.roll(value, 64, 1)).astype(BF16)
            send[a, 2 * m + 1, clip, 2] = halves(pltpu.roll(other, 64, 1), value).astype(BF16)

    @pl.loop(0, CLIPS)
    def _(clip):
        for head in range(2):
            for a, dst in enumerate((q_t, k_t, v_t, c_t)):
                gather(a, clip, head, dst)
            q_n[...] = q_t[...].astype(F32).T.astype(BF16)
            c_n[...] = c_t[...].astype(F32).T.astype(BF16)
            for b in range(SEQ // BLOCK):
                block = slice(b * BLOCK, (b + 1) * BLOCK)
                scores = dot(q_n[block], k_t[...]) * (SCALE * LOG2E)
                low, ds = softmax_grads(scores, dot(c_n[block], v_t[...]))
                to_q = dot(k_t[...], ds, NT)
                for n in range(BLOCK // 128):
                    scatter(0, clip, head, b * (BLOCK // 128) + n, to_q[:, 128 * n:128 * n + 128])
                to_k = dot(q_t[:, block], ds)
                to_v = dot(c_t[:, block], low)
                if b > 0:
                    to_k, to_v = sum_k[...] + to_k, sum_v[...] + to_v
                if b < SEQ // BLOCK - 1:
                    sum_k[...], sum_v[...] = to_k, to_v
            for n in range(SEQ // 128):
                scatter(1, clip, head, n, to_k[:, 128 * n:128 * n + 128])
                scatter(2, clip, head, n, to_v[:, 128 * n:128 * n + 128])
            for slab in (0,) if head == 0 else (1, 2):
                for a in range(3):
                    start_slab(a, clip, slab)

    for clip in range(CLIPS):
        own = [
            pltpu.make_async_copy(send.at[a, ms, clip], recv.at[a, ms, clip], local_sem.at[a])
            for a in range(3)
        ]
        for copy in own:
            copy.start()
        for a, out in enumerate((gq, gk, gv)):
            own[a].wait()

            @pl.loop(1, SPACE)
            def _(i):
                for slab in range(3):
                    copy_of(a, i, clip, slab).wait()

            main = recv[a, :, clip, 0:2].astype(F32).reshape(D, 128)
            out[clip, 0:128, :] = main.T.astype(BF16)
            third = recv[a, :, clip, 2].astype(F32)
            odd = pltpu.roll(third.reshape(SPACE * E, 128), 64, 1).reshape(SPACE, 1, E, 128)
            third = jnp.concatenate([third.reshape(SPACE, 1, E, 128), odd], axis=1).reshape(D, 128)
            out[clip, 128:192, :] = third.T[0:64].astype(BF16)


def on_device(
    q_spatial, k_spatial, v_spatial, q_temporal, k_temporal, v_temporal, grad_out,
    inpaint_mask, frame_order, rel_bias, w_qkv, w_out,
):
    chunks = (FRAMES, GROUPS, 8, D)
    hbm = pl.BlockSpec(memory_space=pl.ANY)
    vmem = pl.BlockSpec(memory_space=pltpu.VMEM)
    smem = pl.BlockSpec(memory_space=pltpu.SMEM)
    dma = pltpu.SemaphoreType.DMA
    slabs = (SPACE, CLIPS, 3, E, 128)
    times = jnp.repeat(frame_order, 8)
    mid, pieces = pl.pallas_call(
        temporal_kernel,
        out_shape=(jax.ShapeDtypeStruct(chunks, BF16), jax.ShapeDtypeStruct((4,) + slabs, BF16)),
        in_specs=[hbm, hbm, hbm, vmem, vmem, vmem, vmem, smem, hbm, hbm, hbm, hbm, hbm],
        out_specs=(vmem, hbm),
        scratch_shapes=[
            pltpu.VMEM(chunks, BF16),
            pltpu.VMEM((4,) + chunks, BF16),
            pltpu.VMEM((4, ROWS, D), BF16),
            pltpu.VMEM((HEADS, ROWS, ROWS), F32),
            pltpu.VMEM((GROUPS * ROWS, 3 * D), BF16),
            pltpu.VMEM(chunks, BF16),
            pltpu.VMEM((3, CLIPS, TOKENS, D), BF16),
            pltpu.VMEM((4,) + slabs, BF16),
            pltpu.VMEM((D, 3 * D), BF16),
            pltpu.VMEM((D, D), BF16),
            dma((4, FRAMES)), dma((4, FRAMES)), dma((FRAMES,)), dma((FRAMES,)),
            dma((4, SPACE)), dma((4, SPACE)), dma((14,)),
        ],
        compiler_params=pltpu.CompilerParams(
            collective_id=0, has_side_effects=True, vmem_limit_bytes=56 * 2**20
        ),
    )(
        q_temporal.reshape(chunks), k_temporal.reshape(chunks), v_temporal.reshape(chunks),
        grad_out.reshape(chunks), inpaint_mask.reshape(FRAMES, GROUPS, 8, 1),
        times.reshape(ROWS, 1), times.reshape(1, ROWS), rel_bias,
        q_spatial.reshape(CLIPS, TOKENS, D), k_spatial.reshape(CLIPS, TOKENS, D),
        v_spatial.reshape(CLIPS, TOKENS, D), w_qkv, w_out,
    )
    shape = (CLIPS, TOKENS, D)
    grads = pl.pallas_call(
        spatial_kernel,
        out_shape=(jax.ShapeDtypeStruct(shape, BF16),) * 3,
        in_specs=[vmem],
        out_specs=(vmem,) * 3,
        scratch_shapes=[
            *(pltpu.VMEM((E, SEQ), BF16) for _ in range(4)),
            *(pltpu.VMEM((SEQ, E), BF16) for _ in range(2)),
            *(pltpu.VMEM((E, SEQ), F32) for _ in range(2)),
            pltpu.VMEM((3, 4, E, 128), F32),
            pltpu.VMEM((3,) + slabs, BF16),
            pltpu.VMEM((3,) + slabs, BF16),
            dma((3, SPACE, CLIPS, 3)), dma((3, SPACE, CLIPS, 3)), dma((3,)),
        ],
        compiler_params=pltpu.CompilerParams(
            collective_id=1, has_side_effects=True, vmem_limit_bytes=56 * 2**20
        ),
    )(pieces)
    full = (CLIPS, 1, TOKENS, D)
    return (*(g.reshape(full) for g in grads), mid.reshape(full))


def solution(mesh):
    split = P(None, "frame", "space", None)
    in_specs = (split,) * 7 + (P(None, "frame", "space"), P(), P(), P(), P())
    return jax.shard_map(
        on_device, mesh=mesh, in_specs=in_specs, out_specs=(split,) * 4, check_vma=False
    )
```

profile of v0, /device:TPU:0, one launch (start us, length us, event | category | flops | bytes accessed | tf_op | source)
XLA Modules:
  0.0 175.4 jit_solution(8734463033652830962)
XLA Ops:
  0.6 0.7 reduce
  1.3 0.7 broadcast_in_dim.3
  2.1 0.6 reshape_reshape.7.fo_row
  2.7 0.7 reshape_reshape.8.fo_col
  3.4 0.9 reshape.56.mask
  4.3 107.0 %shard_map.147 = (bf16[16,3,8,1152]{3,2,1,0:T(8,128)(2,1)}, bf16[4,8,2,3,72,128]{5,4,3,2,1,0:T(8,128)(2,1)}) custom-call(bf16[16,3,8,1152]{3,2,1,0:T(8,128)(2,1)} %bitcast.23, bf16[16,3,8,1152]{3,2,1,0:T(8,128)(2,1)} %bitcast.24, bf16[16,3,8,1152]{3,2,1,0:T(8,128)(2,1)} %bitcast.25, bf16[16,3,8,1152]{3,2,1,0:T(8,128)(2,1)} %bitcast.26, ...), custom_call_target="tpu_custom_call" | custom-call | tf_op jit(solution)/shard_map/pallas_call | solution.py:353
  111.3 57.8 %shard_map.148 = (bf16[2,192,1152]{2,1,0:T(8,128)(2,1)}, bf16[2,192,1152]{2,1,0:T(8,128)(2,1)}, bf16[2,192,1152]{2,1,0:T(8,128)(2,1)}) custom-call(bf16[4,8,2,3,72,128]{5,4,3,2,1,0:T(8,128)(2,1)} %get-tuple-element.9.x), custom_call_target="tpu_custom_call" | custom-call | tf_op jit(solution)/shard_map/pallas_call | solution.py:383
  169.1 0.0 copy-start.1
  169.1 0.0 copy-start
  169.2 2.3 %copy.31 = bf16[2,1,192,1152]{3,2,1,0:T(8,128)(2,1)} copy(bf16[2,1,192,1152]{3,2,1,0:T(8,128)(2,1)} %bitcast.22) | data formatting | bytes 1769472
  171.4 2.1 %copy.32 = bf16[2,1,192,1152]{3,2,1,0:T(8,128)(2,1)} copy(bf16[2,1,192,1152]{3,2,1,0:T(8,128)(2,1)} %bitcast.21) | data formatting | bytes 1769472
  173.6 0.0 copy-done.1
  173.6 0.9 copy.33
  174.5 0.0 copy-done
  174.5 0.9 copy.34
Async XLA Ops:
  169.1 4.4 %copy-start.1 = (bf16[2,192,1152]{2,1,0:T(8,128)(2,1)S(1)}, bf16[2,192,1152]{2,1,0:T(8,128)(2,1)}, u32[]{:S(2)}) copy-start(bf16[2,192,1152]{2,1,0:T(8,128)(2,1)} %get-tuple-element.12) | copy-start | bytes 2654212
  169.1 5.3 %copy-start = (bf16[16,3,8,1152]{3,2,1,0:T(8,128)(2,1)S(1)}, bf16[16,3,8,1152]{3,2,1,0:T(8,128)(2,1)}, u32[]{:S(2)}) copy-start(bf16[16,3,8,1152]{3,2,1,0:T(8,128)(2,1)} %get-tuple-element.13) | copy-start | bytes 2654212
where the time goes:
time: 176 us; the launch traced here: 175 us
  Pallas kernels  165 us (94%)
  local copies, waits for them, and re-layouts  9.17 us (5%)
    pallas_call x1, Pallas kernels, on_device(): pl.pallas_call(temporal_kernel, out_shape=(jax.ShapeDtypeStruct(chunks, B...  107 us
    pallas_call x1, Pallas kernels, on_device(): pl.pallas_call(spatial_kernel, out_shape=(jax.ShapeDtypeStruct(shape, BF1...  57.8 us
    unnamed x8, local copies, waits for them, and re-layouts  6.25 us

commit v1 on v0

v1 whole, which is shorter than its diff:
```python
import jax
import jax.numpy as jnp
from jax import lax
from jax.experimental import pallas as pl
from jax.experimental.pallas import tpu as pltpu
from jax.sharding import PartitionSpec as P

HEADS = 16
E = 72
D = 1152
CLIPS = 2
FRAMES = 16
TOKENS = 192
SEQ = 1536
SPACE = 8
GROUPS = 3
ROWS = 128
BLOCK = 512
SCALE = E ** (-0.5)
LOG2E = 1.4426950408889634
MESH = pl.DeviceIdType.MESH
NN = (((1,), (0,)), ((), ()))
NT = (((1,), (1,)), ((), ()))
F32 = jnp.float32
BF16 = jnp.bfloat16


def dot(a, b, dims=NN):
    return lax.dot_general(a, b, dims, preferred_element_type=F32)


def softmax(scores):
    weights = jnp.exp2(scores - jnp.max(scores, axis=1, keepdims=True))
    return weights * (1.0 / jnp.sum(weights, axis=1, keepdims=True))


def score_grads(probs, probs_low, dprob):
    delta = jnp.sum(probs_low.astype(F32) * dprob, axis=1, keepdims=True)
    return (probs * (dprob - delta)).astype(BF16)


def halves(low, high):
    lane = lax.broadcasted_iota(jnp.int32, low.shape, 1)
    return jnp.where(lane < 64, low, high)


def store_slabs(dst, main0, main1, third):
    for clip, main in enumerate((main0, main1)):
        by_head = main.reshape(SPACE, 2, E, 128)
        dst[:, clip, 0] = by_head[:, 0].astype(BF16)
        dst[:, clip, 1] = by_head[:, 1].astype(BF16)
    by_head = third.reshape(SPACE, 2, E, 128)
    even = by_head[:, 0].reshape(SPACE * E, 128)
    odd = by_head[:, 1].reshape(SPACE * E, 128)
    dst[:, 0, 2] = halves(even, pltpu.roll(odd, 64, 1)).reshape(SPACE, E, 128).astype(BF16)
    dst[:, 1, 2] = halves(pltpu.roll(even, 64, 1), odd).reshape(SPACE, E, 128).astype(BF16)


def kernel(
    qt, kt, vt, go, mask, order, rel_bias, qs, ks, vs, wqkv, wout,
    gq, gk, gv, gm,
    cot, tin, xg, bias, joined, gm_send, gm_in, sin, send, recv, back, wq, wo,
    probs, q_t, k_t, v_t, c_t, row_n, sum_k, sum_v, thirds,
    t_send_sem, t_recv_sem, g_send_sem, g_recv_sem, s_send_sem, s_recv_sem, b_send_sem, b_recv_sem,
    local_sem, own_sem, out_sem,
):
    mf, ms = lax.axis_index("frame"), lax.axis_index("space")
    loads = [
        pltpu.make_async_copy(src, dst, local_sem.at[n])
        for n, (src, dst) in enumerate(
            ((go, sin.at[3]), (qs, sin.at[0]), (ks, sin.at[1]), (vs, sin.at[2]), (wqkv, wq), (wout, wo))
        )
    ]
    for copy in loads:
        copy.start()

    barrier = pltpu.get_barrier_semaphore()

    @pl.loop(1, FRAMES)
    def _(i):
        pl.semaphore_signal(barrier, inc=1, device_id=(lax.rem(mf + i, FRAMES), ms), device_id_type=MESH)

    @pl.loop(1, SPACE)
    def _(i):
        pl.semaphore_signal(barrier, inc=1, device_id=(mf, lax.rem(ms + i, SPACE)), device_id_type=MESH)

    pl.semaphore_wait(barrier, FRAMES + SPACE - 2)

    sources = (qt, kt, cot, vt)

    def t_copy(a, i):
        peer = lax.rem(mf + i, FRAMES)
        return pltpu.make_async_remote_copy(
            src_ref=sources[a].at[peer], dst_ref=tin.at[a, mf],
            send_sem=t_send_sem.at[a, i], recv_sem=t_recv_sem.at[a, i],
            device_id=(peer, ms), device_id_type=MESH,
        )

    def g_copy(i):
        peer = lax.rem(mf + i, FRAMES)
        return pltpu.make_async_remote_copy(
            src_ref=gm_send.at[peer], dst_ref=gm_in.at[mf],
            send_sem=g_send_sem.at[i], recv_sem=g_recv_sem.at[i],
            device_id=(peer, ms), device_id_type=MESH,
        )

    def s_copy(a, i, clip):
        peer = lax.rem(ms + i, SPACE)
        return pltpu.make_async_remote_copy(
            src_ref=send.at[a, peer, clip], dst_ref=recv.at[a, ms, clip],
            send_sem=s_send_sem.at[a, i, clip], recv_sem=s_recv_sem.at[a, i, clip],
            device_id=(mf, peer), device_id_type=MESH,
        )

    def own_copy(a, clip):
        return pltpu.make_async_copy(send.at[a, ms, clip], recv.at[a, ms, clip], own_sem.at[a, clip])

    def s_wait(a, clip):
        own_copy(a, clip).wait()

        @pl.loop(1, SPACE)
        def _(i):
            s_copy(a, i, clip).wait()

    def b_copy(a, i, clip, slab):
        peer = lax.rem(ms + i, SPACE)
        return pltpu.make_async_remote_copy(
            src_ref=send.at[a, peer, clip, slab], dst_ref=back.at[a, ms, clip, slab],
            send_sem=b_send_sem.at[a, i, clip, slab], recv_sem=b_recv_sem.at[a, i, clip, slab],
            device_id=(mf, peer), device_id_type=MESH,
        )

    def t_start(a):
        @pl.loop(1, FRAMES)
        def _(i):
            t_copy(a, i).start()

    t_start(0)
    t_start(1)
    loads[0].wait()
    row = lax.broadcasted_iota(jnp.int32, (TOKENS, TOKENS), 0)
    col = lax.broadcasted_iota(jnp.int32, (TOKENS, TOKENS), 1)
    for clip in range(CLIPS):
        diagonal = jnp.where(row == col, mask[clip].astype(F32), 0.0).astype(BF16)
        masked = dot(diagonal, sin[3, clip])
        cot[8 * clip:8 * clip + 8] = masked.reshape(8, GROUPS, 8, D).astype(BF16)
    t_start(2)
    t_start(3)
    own = [
        pltpu.make_async_copy(sources[a].at[mf], tin.at[a, mf], local_sem.at[6 + a]) for a in range(4)
    ]
    for copy in own:
        copy.start()

    for a in range(3):
        loads[1 + a].wait()

    @pl.loop(0, 3)
    def _(a):
        x = sin.at[a]
        main0 = x[0, 0:128, :].astype(F32).T
        main1 = x[1, 0:128, :].astype(F32).T
        third = jnp.concatenate([x[0, 128:192, :].astype(F32), x[1, 128:192, :].astype(F32)], axis=0).T
        store_slabs(send.at[a], main0, main1, third)
        for clip in range(CLIPS):
            own_copy(a, clip).start()
            for i in (2, 4, 6):
                s_copy(a, i, clip).start()

    row = lax.broadcasted_iota(jnp.int32, (ROWS, ROWS), 0)
    col = lax.broadcasted_iota(jnp.int32, (ROWS, ROWS), 1)
    offset = jnp.full((ROWS, ROWS), FRAMES - 1, jnp.int32)
    for f in range(FRAMES):
        offset = offset + jnp.where((row >> 3) == f, order[f], 0) - jnp.where((col >> 3) == f, order[f], 0)
    offset = jnp.where((row & 7) == (col & 7), offset, -1)

    @pl.loop(0, HEADS)
    def _(h):
        total = jnp.full((ROWS, ROWS), -1e30, F32)
        for o in range(2 * FRAMES - 1):
            total = jnp.where(offset == o, rel_bias[h, o] * LOG2E, total)
        bias[h] = total

    for a in range(4):
        own[a].wait()

        @pl.loop(1, FRAMES)
        def _(i):
            t_copy(a, i).wait()

    for a in range(2):
        for clip in range(CLIPS):
            for i in (1, 7, 3, 5):
                s_copy(a, i, clip).start()

    lane = lax.broadcasted_iota(jnp.int32, (1, 256), 1)

    @pl.loop(0, GROUPS)
    def _(g):
        for a in range(4):
            xg[a] = tin[a, :, g].astype(F32).reshape(ROWS, D).astype(BF16)
        carry = None
        for p in range(SPACE):
            window = slice(128 * p, 128 * p + 256)
            first = 16 * p
            m0 = jnp.where((lane >= first) & (lane < first + E), 1.0, 0.0).astype(BF16)
            m1 = jnp.where((lane >= first + E) & (lane < first + 2 * E), 1.0, 0.0).astype(BF16)

            def stacked(x):
                return jnp.concatenate([x * m0, x * m1], axis=0)

            q, k, c, v = (xg[a, :, window] for a in range(4))
            k2 = stacked(k)
            scores = dot(q, k2, NT)
            dprob = dot(c, stacked(v), NT)
            ds, low_t, ds_t = [], [], []
            for n in range(2):
                part = slice(128 * n, 128 * n + 128)
                pr = softmax(scores[:, part] * (SCALE * LOG2E) + bias[2 * p + n])
                low = pr.astype(BF16)
                d = score_grads(pr, low, dprob[:, part])
                ds.append(d)
                low_t.append(low.astype(F32).T.astype(BF16))
                ds_t.append(d.astype(F32).T.astype(BF16))
            outs = (
                dot(jnp.concatenate(ds, axis=1), k2) * SCALE,
                dot(jnp.concatenate(ds_t, axis=1), stacked(q)) * SCALE,
                dot(jnp.concatenate(low_t, axis=1), stacked(c)),
            )
            rows = pl.ds(pl.multiple_of(g * ROWS, ROWS), ROWS)
            for n, out in enumerate(outs):
                left = out[:, :128] if carry is None else out[:, :128] + carry[n]
                joined[rows, D * n + 128 * p:D * n + 128 * p + 128] = left.astype(BF16)
                if p == SPACE - 1:
                    joined[rows, D * n + 1024:D * n + D] = out[:, 128:].astype(BF16)
            carry = [out[:, 128:] for out in outs]

    loads[4].wait()
    mid = dot(joined[...], wq[...], NT)
    for g in range(GROUPS):
        gm_send[:, g] = mid[g * ROWS:(g + 1) * ROWS].reshape(FRAMES, 8, D).astype(BF16)

    @pl.loop(1, FRAMES)
    def _(i):
        g_copy(i).start()

    own_gm = pltpu.make_async_copy(gm_send.at[mf], gm_in.at[mf], local_sem.at[10])
    own_gm.start()
    for i in (1, 7, 3, 5):
        s_copy(2, i, 0).start()
    own_gm.wait()

    @pl.loop(1, FRAMES)
    def _(i):
        g_copy(i).wait()

    gm_out = pltpu.make_async_copy(gm_in, gm, local_sem.at[11])
    gm_out.start()
    loads[5].wait()
    mid = gm_in[...].astype(F32).reshape(CLIPS, TOKENS, D)
    mid = jnp.concatenate([mid[0, :128], mid[1, :128], mid[0, 128:], mid[1, 128:]], axis=0).astype(BF16)
    cot_t = dot(wo[...], mid, NT)
    store_slabs(send.at[3], cot_t[:, :128], cot_t[:, 128:256], cot_t[:, 256:])
    for clip in range(CLIPS):
        if clip == 1:
            for i in (1, 7, 3, 5):
                s_copy(2, i, 1).start()
        own_copy(3, clip).start()
        for i in (1, 7, 3, 5, 2, 4, 6):
            s_copy(3, i, clip).start()

    def gather(a, clip, head, dst):
        for s in range(SPACE):
            dst[:, 128 * s:128 * s + 128] = recv[a, s, clip, head]
        for m in range(SPACE // 2):
            low = recv[a, 2 * m, clip, 2].astype(F32)
            high = recv[a, 2 * m + 1, clip, 2].astype(F32)
            if head == 0:
                high = pltpu.roll(high, 64, 1)
            else:
                low = pltpu.roll(low, 64, 1)
            dst[:, 1024 + 128 * m:1152 + 128 * m] = halves(low, high).astype(BF16)

    @pl.loop(0, CLIPS)
    def _(clip):
        s_wait(0, clip)
        s_wait(1, clip)
        for head in range(2):
            gather(0, clip, head, q_t)
            gather(1, clip, head, k_t)
            row_n[...] = q_t[...].astype(F32).T.astype(BF16)
            for b in range(SEQ // BLOCK):
                block = slice(b * BLOCK, (b + 1) * BLOCK)
                scores = dot(row_n[block], k_t[...]) * (SCALE * LOG2E)
                probs[2 * clip + head, block] = softmax(scores).astype(BF16)

    def scatter(a, clip, head, tile, value):
        if tile < SPACE:
            send[a, tile, clip, head] = value.astype(BF16)
        elif head == 0:
            thirds[a, tile - SPACE] = value
        else:
            m = tile - SPACE
            other = thirds[a, m]
            send[a, 2 * m, clip, 2] = halves(other, pltpu.roll(value, 64, 1)).astype(BF16)
            send[a, 2 * m + 1, clip, 2] = halves(pltpu.roll(other, 64, 1), value).astype(BF16)

    @pl.loop(0, CLIPS)
    def _(clip):
        s_wait(2, clip)
        s_wait(3, clip)
        for head in range(2):
            for a, dst in enumerate((q_t, k_t, v_t, c_t)):
                gather(a, clip, head, dst)
            row_n[...] = c_t[...].astype(F32).T.astype(BF16)
            for b in range(SEQ // BLOCK):
                block = slice(b * BLOCK, (b + 1) * BLOCK)
                low = probs[2 * clip + head, block]
                ds = score_grads(low.astype(F32), low, dot(row_n[block], v_t[...]))
                to_q = dot(k_t[...], ds, NT) * SCALE
                for n in range(BLOCK // 128):
                    scatter(0, clip, head, b * (BLOCK // 128) + n, to_q[:, 128 * n:128 * n + 128])
                to_k = dot(q_t[:, block], ds)
                to_v = dot(c_t[:, block], low)
                if b > 0:
                    to_k, to_v = sum_k[...] + to_k, sum_v[...] + to_v
                if b < SEQ // BLOCK - 1:
                    sum_k[...], sum_v[...] = to_k, to_v
            to_k = to_k * SCALE
            for n in range(SEQ // 128):
                scatter(1, clip, head, n, to_k[:, 128 * n:128 * n + 128])
                scatter(2, clip, head, n, to_v[:, 128 * n:128 * n + 128])
            for slab in (0,) if head == 0 else (1, 2):
                for a in range(3):
                    for i in (1, 7, 3, 5, 2, 4, 6):
                        b_copy(a, i, clip, slab).start()

    outs = []
    for clip in range(CLIPS):
        own = [
            pltpu.make_async_copy(send.at[a, ms, clip], back.at[a, ms, clip], local_sem.at[a])
            for a in range(3)
        ]
        for copy in own:
            copy.start()
        for a, out in enumerate((gq, gk, gv)):
            own[a].wait()

            @pl.loop(1, SPACE)
            def _(i):
                for slab in range(3):
                    b_copy(a, i, clip, slab).wait()

            main = back[a, :, clip, 0:2].astype(F32).reshape(D, 128)
            sin[a, clip, 0:128, :] = main.T.astype(BF16)
            third = back[a, :, clip, 2].astype(F32)
            odd = pltpu.roll(third.reshape(SPACE * E, 128), 64, 1).reshape(SPACE, 1, E, 128)
            third = jnp.concatenate([third.reshape(SPACE, 1, E, 128), odd], axis=1).reshape(D, 128)
            sin[a, clip, 128:192, :] = third.T[0:64].astype(BF16)
            outs.append(pltpu.make_async_copy(sin.at[a, clip], out.at[clip], out_sem.at[a, clip]))
            outs[-1].start()
    gm_out.wait()
    for copy in outs:
        copy.wait()


def copy_kernel(a, b, c, d, a_out, b_out, c_out, d_out, sem):
    copies = []
    for n, (src, dst) in enumerate(((a, a_out), (b, b_out), (c, c_out), (d, d_out))):
        for part in range(4):
            rows = pl.ds(96 * part, 96)
            copies.append(pltpu.make_async_copy(src.at[rows], dst.at[rows], sem.at[n, part]))
            copies[-1].start()
    for copy in copies:
        copy.wait()


def on_device(
    q_spatial, k_spatial, v_spatial, q_temporal, k_temporal, v_temporal, grad_out,
    inpaint_mask, frame_order, rel_bias, w_qkv, w_out,
):
    chunks = (FRAMES, GROUPS, 8, D)
    shape = (CLIPS, TOKENS, D)
    slabs = (SPACE, CLIPS, 3, E, 128)
    hbm = pl.BlockSpec(memory_space=pl.ANY)
    vmem = pl.BlockSpec(memory_space=pltpu.VMEM)
    smem = pl.BlockSpec(memory_space=pltpu.SMEM)
    dma = pltpu.SemaphoreType.DMA
    results = pl.pallas_call(
        kernel,
        out_shape=(jax.ShapeDtypeStruct(shape, BF16),) * 3 + (jax.ShapeDtypeStruct(chunks, BF16),),
        in_specs=[hbm, hbm, hbm, hbm, vmem, smem, smem, hbm, hbm, hbm, hbm, hbm],
        out_specs=(hbm,) * 4,
        scratch_shapes=[
            pltpu.VMEM(chunks, BF16),
            pltpu.VMEM((4,) + chunks, BF16),
            pltpu.VMEM((4, ROWS, D), BF16),
            pltpu.VMEM((HEADS, ROWS, ROWS), F32),
            pltpu.VMEM((GROUPS * ROWS, 3 * D), BF16),
            pltpu.VMEM(chunks, BF16),
            pltpu.VMEM(chunks, BF16),
            pltpu.VMEM((4,) + shape, BF16),
            pltpu.VMEM((4,) + slabs, BF16),
            pltpu.VMEM((4,) + slabs, BF16),
            pltpu.VMEM((3,) + slabs, BF16),
            pltpu.VMEM((D, 3 * D), BF16),
            pltpu.VMEM((D, D), BF16),
            pltpu.VMEM((4, SEQ, SEQ), BF16),
            *(pltpu.VMEM((E, SEQ), BF16) for _ in range(4)),
            pltpu.VMEM((SEQ, E), BF16),
            *(pltpu.VMEM((E, SEQ), F32) for _ in range(2)),
            pltpu.VMEM((3, 4, E, 128), F32),
            dma((4, FRAMES)), dma((4, FRAMES)), dma((FRAMES,)), dma((FRAMES,)),
            dma((4, SPACE, CLIPS)), dma((4, SPACE, CLIPS)),
            dma((3, SPACE, CLIPS, 3)), dma((3, SPACE, CLIPS, 3)),
            dma((12,)), dma((4, CLIPS)), dma((3, CLIPS)),
        ],
        compiler_params=pltpu.CompilerParams(
            collective_id=0, has_side_effects=True, vmem_limit_bytes=63 * 2**20
        ),
    )(
        q_temporal.reshape(chunks), k_temporal.reshape(chunks), v_temporal.reshape(chunks),
        grad_out.reshape(shape), inpaint_mask, frame_order, rel_bias,
        q_spatial.reshape(shape), k_spatial.reshape(shape), v_spatial.reshape(shape), w_qkv, w_out,
    )
    flat = (CLIPS * TOKENS, D)
    results = pl.pallas_call(
        copy_kernel,
        out_shape=(jax.ShapeDtypeStruct(flat, BF16),) * 4,
        in_specs=[hbm] * 4,
        out_specs=(hbm,) * 4,
        scratch_shapes=[dma((4, 4))],
    )(*(r.reshape(flat) for r in results))
    return tuple(r.reshape(CLIPS, 1, TOKENS, D) for r in results)


def solution(mesh):
    split = P(None, "frame", "space", None)
    in_specs = (split,) * 7 + (P(None, "frame", "space"), P(), P(), P(), P())
    return jax.shard_map(
        on_device, mesh=mesh, in_specs=in_specs, out_specs=(split,) * 4, check_vma=False
    )
```

time: 176 us -> 254 us (1.44)
  Pallas kernels: 165 us -> 253 us
  local copies, waits for them, and re-layouts: 9.17 us -> 0 us
    pallas_call x2, Pallas kernels: 165 us -> 253 us  [the longest x1 145 us: on_device(): pl.pallas_call(kernel, out_shape=(jax.ShapeDtypeStruct(shape, BF16),) * 3...]
    unnamed x8 -> x0, local copies, waits for them, and re-layouts: 6.25 us -> none
where the time goes in v1:
time: 254 us
  Pallas kernels  253 us (100%)
    pallas_call x1, Pallas kernels, on_device(): pl.pallas_call(kernel, out_shape=(jax.ShapeDtypeStruct(shape, BF16),) * 3...  145 us
    pallas_call x1, Pallas kernels, on_device(): pl.pallas_call(copy_kernel, out_shape=(jax.ShapeDtypeStruct(flat, BF16),)...  108 us

profile of v1, /device:TPU:0, one launch (start us, length us, event | category | flops | bytes accessed | tf_op | source)
XLA Modules:
  0.0 254.0 jit_solution(929850422570368334)
XLA Ops:
  0.6 144.7 %shard_map.147 = (bf16[2,192,1152]{2,1,0:T(8,128)(2,1)}, bf16[2,192,1152]{2,1,0:T(8,128)(2,1)}, bf16[2,192,1152]{2,1,0:T(8,128)(2,1)}, bf16[16,3,8,1152]{3,2,1,0:T(8,128)(2,1)}) custom-call(bf16[16,3,8,1152]{3,2,1,0:T(8,128)(2,1)} %bitcast.27, bf16[16,3,8,1152]{3,2,1,0:T(8,128)(2,1)} %bitcast.28, bf16[16,3,8,1152]{3,2,1,0:T(8,128)(2,1)} %bitcast.29, ...), custom_call_target="tpu_custom_call" | custom-call | tf_op jit(solution)/shard_map/pallas_call | solution.py:389
  145.4 108.5 %shard_map.148 = (bf16[384,1152]{1,0:T(8,128)(2,1)}, bf16[384,1152]{1,0:T(8,128)(2,1)}, bf16[384,1152]{1,0:T(8,128)(2,1)}, bf16[384,1152]{1,0:T(8,128)(2,1)}) custom-call(bf16[384,1152]{1,0:T(8,128)(2,1)} %bitcast.23, bf16[384,1152]{1,0:T(8,128)(2,1)} %bitcast.24, bf16[384,1152]{1,0:T(8,128)(2,1)} %bitcast.25, bf16[384,1152]{1,0:T(8,128)(2,1)} %bitcast.26), custom_call_target="tpu_custom_call" | custom-call | tf_op jit(solution)/shard_map/pallas_call | solution.py:427

commit v2 on v1

--- a/solution.py
+++ b/solution.py
@@ -364,14 +364,16 @@
         copy.wait()
 
 
-def copy_kernel(a, b, c, d, a_out, b_out, c_out, d_out, sem):
-    copies = []
-    for n, (src, dst) in enumerate(((a, a_out), (b, b_out), (c, c_out), (d, d_out))):
-        for part in range(4):
-            rows = pl.ds(96 * part, 96)
-            copies.append(pltpu.make_async_copy(src.at[rows], dst.at[rows], sem.at[n, part]))
-            copies[-1].start()
-    for copy in copies:
+def copy_kernel(a, b, c, d, a_out, b_out, c_out, d_out, held, in_sem, out_sem):
+    pairs = ((a, a_out), (b, b_out), (c, c_out), (d, d_out))
+    reads = [pltpu.make_async_copy(src, held.at[n], in_sem.at[n]) for n, (src, _) in enumerate(pairs)]
+    writes = [pltpu.make_async_copy(held.at[n], dst, out_sem.at[n]) for n, (_, dst) in enumerate(pairs)]
+    for copy in reads:
+        copy.start()
+    for read, write in zip(reads, writes):
+        read.wait()
+        write.start()
+    for copy in writes:
         copy.wait()
 
 
@@ -429,7 +431,7 @@
         out_shape=(jax.ShapeDtypeStruct(flat, BF16),) * 4,
         in_specs=[hbm] * 4,
         out_specs=(hbm,) * 4,
-        scratch_shapes=[dma((4, 4))],
+        scratch_shapes=[pltpu.VMEM((4,) + flat, BF16), dma((4,)), dma((4,))],
     )(*(r.reshape(flat) for r in results))
     return tuple(r.reshape(CLIPS, 1, TOKENS, D) for r in results)
 

time: 254 us -> 149 us (0.59)
  Pallas kernels: 253 us -> 148 us
    pallas_call x1, Pallas kernels: 108 us -> 3.02 us  [on_device(): pl.pallas_call(copy_kernel, out_shape=(jax.ShapeDtypeStruct(flat, BF16),)...]
where the time goes in v2:
time: 149 us
  Pallas kernels  148 us (99%)
    pallas_call x1, Pallas kernels, on_device(): pl.pallas_call(kernel, out_shape=(jax.ShapeDtypeStruct(shape, BF16),) * 3...  145 us
    pallas_call x1, Pallas kernels, on_device(): pl.pallas_call(copy_kernel, out_shape=(jax.ShapeDtypeStruct(flat, BF16),)...  3.02 us

profile of v2, /device:TPU:0, one launch (start us, length us, event | category | flops | bytes accessed | tf_op | source)
XLA Modules:
  0.0 148.6 jit_solution(12722069984838749887)
XLA Ops:
  0.6 144.7 %shard_map.147 = (bf16[2,192,1152]{2,1,0:T(8,128)(2,1)}, bf16[2,192,1152]{2,1,0:T(8,128)(2,1)}, bf16[2,192,1152]{2,1,0:T(8,128)(2,1)}, bf16[16,3,8,1152]{3,2,1,0:T(8,128)(2,1)}) custom-call(bf16[16,3,8,1152]{3,2,1,0:T(8,128)(2,1)} %bitcast.27, bf16[16,3,8,1152]{3,2,1,0:T(8,128)(2,1)} %bitcast.28, bf16[16,3,8,1152]{3,2,1,0:T(8,128)(2,1)} %bitcast.29, ...), custom_call_target="tpu_custom_call" | custom-call | tf_op jit(solution)/shard_map/pallas_call | solution.py:391
  145.4 3.0 %shard_map.148 = (bf16[384,1152]{1,0:T(8,128)(2,1)}, bf16[384,1152]{1,0:T(8,128)(2,1)}, bf16[384,1152]{1,0:T(8,128)(2,1)}, bf16[384,1152]{1,0:T(8,128)(2,1)}) custom-call(bf16[384,1152]{1,0:T(8,128)(2,1)} %bitcast.23, bf16[384,1152]{1,0:T(8,128)(2,1)} %bitcast.24, bf16[384,1152]{1,0:T(8,128)(2,1)} %bitcast.25, bf16[384,1152]{1,0:T(8,128)(2,1)} %bitcast.26), custom_call_target="tpu_custom_call" | custom-call | tf_op jit(solution)/shard_map/pallas_call | solution.py:429

commit v3 on v2

v3 whole, which is shorter than its diff:
```python
import jax
import jax.numpy as jnp
from jax import lax
from jax.experimental import pallas as pl
from jax.experimental.pallas import tpu as pltpu
from jax.sharding import PartitionSpec as P

HEADS = 16
E = 72
D = 1152
CLIPS = 2
FRAMES = 16
TOKENS = 192
SEQ = 1536
SPACE = 8
GROUPS = 3
ROWS = 128
BLOCK = 512
SCALE = E ** (-0.5)
LOG2E = 1.4426950408889634
MESH = pl.DeviceIdType.MESH
NN = (((1,), (0,)), ((), ()))
NT = (((1,), (1,)), ((), ()))
F32 = jnp.float32
BF16 = jnp.bfloat16


def dot(a, b, dims=NN):
    return lax.dot_general(a, b, dims, preferred_element_type=F32)


def softmax(scores):
    weights = jnp.exp2(scores - jnp.max(scores, axis=1, keepdims=True))
    return weights * (1.0 / jnp.sum(weights, axis=1, keepdims=True))


def score_grads(probs, probs_low, dprob):
    delta = jnp.sum(probs_low.astype(F32) * dprob, axis=1, keepdims=True)
    return (probs * (dprob - delta)).astype(BF16)


def halves(low, high):
    lane = lax.broadcasted_iota(jnp.int32, low.shape, 1)
    return jnp.where(lane < 64, low, high)


def store_slabs(dst, main0, main1, third):
    for clip, main in enumerate((main0, main1)):
        by_head = main.reshape(SPACE, 2, E, 128)
        dst[:, clip, 0] = by_head[:, 0].astype(BF16)
        dst[:, clip, 1] = by_head[:, 1].astype(BF16)
    by_head = third.reshape(SPACE, 2, E, 128)
    even = by_head[:, 0].reshape(SPACE * E, 128)
    odd = by_head[:, 1].reshape(SPACE * E, 128)
    dst[:, 0, 2] = halves(even, pltpu.roll(odd, 64, 1)).reshape(SPACE, E, 128).astype(BF16)
    dst[:, 1, 2] = halves(pltpu.roll(even, 64, 1), odd).reshape(SPACE, E, 128).astype(BF16)


def kernel(
    qt, kt, vt, go, mask, order, rel_bias, qs, ks, vs, wqkv, wout,
    gq, gk, gv, gm,
    cot, tin, bias, joined, gm_in, sin, send, recv, back, wq, wo,
    probs, q_t, k_t, v_t, c_t, row_n, sum_k, sum_v, thirds,
    t_send_sem, t_recv_sem, g_send_sem, g_recv_sem, s_send_sem, s_recv_sem, b_send_sem, b_recv_sem,
    local_sem, own_sem, out_sem,
):
    mf, ms = lax.axis_index("frame"), lax.axis_index("space")
    barrier = pltpu.get_barrier_semaphore()

    @pl.loop(1, FRAMES)
    def _(i):
        pl.semaphore_signal(barrier, inc=1, device_id=(lax.rem(mf + i, FRAMES), ms), device_id_type=MESH)

    @pl.loop(1, SPACE)
    def _(i):
        pl.semaphore_signal(barrier, inc=1, device_id=(mf, lax.rem(ms + i, SPACE)), device_id_type=MESH)

    loads = [
        pltpu.make_async_copy(src, dst, local_sem.at[n])
        for n, (src, dst) in enumerate(
            ((go, cot), (qs, sin.at[0]), (ks, sin.at[1]), (vs, sin.at[2]), (wqkv, wq), (wout, wo))
        )
    ]
    loads[0].start()
    pl.semaphore_wait(barrier, FRAMES + SPACE - 2)

    sources = (qt, kt, cot, vt)

    def t_start(a, g):
        @pl.loop(1, FRAMES)
        def _(i):
            peer = lax.rem(mf + i, FRAMES)
            pltpu.make_async_remote_copy(
                src_ref=sources[a].at[peer, g], dst_ref=tin.at[a, mf, g],
                send_sem=t_send_sem.at[a, g], recv_sem=t_recv_sem.at[a, g],
                device_id=(peer, ms), device_id_type=MESH,
            ).start()
        pltpu.make_async_copy(sources[a].at[mf, g], tin.at[a, mf, g], own_sem.at[a, g]).start()

    def t_wait(a, g):
        some = tin.at[a, 0:FRAMES - 1, g]
        sems = (t_send_sem.at[a, g], t_recv_sem.at[a, g])
        pltpu.make_async_copy(sources[a].at[mf, g], tin.at[a, mf, g], own_sem.at[a, g]).wait()
        for sem in sems:
            pltpu.make_async_copy(some, some, sem).wait()

    def g_start(g):
        @pl.loop(1, FRAMES)
        def _(i):
            peer = lax.rem(mf + i, FRAMES)
            pltpu.make_async_remote_copy(
                src_ref=tin.at[0, peer, g], dst_ref=gm_in.at[mf, g],
                send_sem=g_send_sem.at[g], recv_sem=g_recv_sem.at[g],
                device_id=(peer, ms), device_id_type=MESH,
            ).start()
        pltpu.make_async_copy(tin.at[0, mf, g], gm_in.at[mf, g], own_sem.at[4, g]).start()

    def g_wait(g):
        some = gm_in.at[0:FRAMES - 1, g]
        sems = (g_send_sem.at[g], g_recv_sem.at[g])
        pltpu.make_async_copy(tin.at[0, mf, g], gm_in.at[mf, g], own_sem.at[4, g]).wait()
        for sem in sems:
            pltpu.make_async_copy(some, some, sem).wait()

    def s_start(a, clip):
        pltpu.make_async_copy(send.at[a, ms, clip], recv.at[a, ms, clip], own_sem.at[5 + a, clip]).start()
        for i in (1, 7, 3, 5, 2, 4, 6):
            peer = lax.rem(ms + i, SPACE)
            pltpu.make_async_remote_copy(
                src_ref=send.at[a, peer, clip], dst_ref=recv.at[a, ms, clip],
                send_sem=s_send_sem.at[a, clip], recv_sem=s_recv_sem.at[a, clip],
                device_id=(mf, peer), device_id_type=MESH,
            ).start()

    def s_wait(a, clip):
        some = recv.at[a, 0:SPACE - 1, clip]
        sems = (s_send_sem.at[a, clip], s_recv_sem.at[a, clip])
        pltpu.make_async_copy(send.at[a, ms, clip], recv.at[a, ms, clip], own_sem.at[5 + a, clip]).wait()
        for sem in sems:
            pltpu.make_async_copy(some, some, sem).wait()

    def b_start(a, peer, clip, slab):
        @pl.when(peer != ms)
        def _():
            pltpu.make_async_remote_copy(
                src_ref=send.at[a, peer, clip, slab], dst_ref=back.at[a, ms, clip, slab],
                send_sem=b_send_sem.at[a, clip], recv_sem=b_recv_sem.at[a, clip],
                device_id=(mf, peer), device_id_type=MESH,
            ).start()

    def b_start_all(a, clip, slab):
        for i in (1, 7, 3, 5, 2, 4, 6):
            peer = lax.rem(ms + i, SPACE)
            pltpu.make_async_remote_copy(
                src_ref=send.at[a, peer, clip, slab], dst_ref=back.at[a, ms, clip, slab],
                send_sem=b_send_sem.at[a, clip], recv_sem=b_recv_sem.at[a, clip],
                device_id=(mf, peer), device_id_type=MESH,
            ).start()

    def b_wait(a, clip):
        some = back.at[a, 0:SPACE - 1, clip]
        sems = (b_send_sem.at[a, clip], b_recv_sem.at[a, clip])
        for sem in sems:
            pltpu.make_async_copy(some, some, sem).wait()

    t_start(0, 0)
    t_start(1, 0)
    t_start(3, 0)
    loads[0].wait()
    row = lax.broadcasted_iota(jnp.int32, (TOKENS, TOKENS), 0)
    col = lax.broadcasted_iota(jnp.int32, (TOKENS, TOKENS), 1)
    for clip in range(CLIPS):
        diagonal = jnp.where(row == col, mask[clip].astype(F32), 0.0).astype(BF16)
        masked = dot(diagonal, cot[8 * clip:8 * clip + 8].astype(F32).reshape(TOKENS, D).astype(BF16))
        cot[8 * clip:8 * clip + 8] = masked.reshape(8, GROUPS, 8, D).astype(BF16)
    t_start(2, 0)
    for g in range(1, GROUPS):
        for a in range(4):
            t_start(a, g)
    for copy in loads[1:]:
        copy.start()

    row = lax.broadcasted_iota(jnp.int32, (ROWS, ROWS), 0)
    col = lax.broadcasted_iota(jnp.int32, (ROWS, ROWS), 1)
    offset = jnp.full((ROWS, ROWS), FRAMES - 1, jnp.int32)
    for f in range(FRAMES):
        offset = offset + jnp.where((row >> 3) == f, order[f], 0) - jnp.where((col >> 3) == f, order[f], 0)
    offset = jnp.where((row & 7) == (col & 7), offset, -1)

    @pl.loop(0, HEADS)
    def _(h):
        total = jnp.full((ROWS, ROWS), -1e30, F32)
        for o in range(2 * FRAMES - 1):
            total = jnp.where(offset == o, rel_bias[h, o] * LOG2E, total)
        bias[h] = total

    for copy in loads[1:]:
        copy.wait()

    @pl.loop(0, 3)
    def _(a):
        x = sin.at[a]
        main0 = x[0, 0:128, :].astype(F32).T
        main1 = x[1, 0:128, :].astype(F32).T
        third = jnp.concatenate([x[0, 128:192, :].astype(F32), x[1, 128:192, :].astype(F32)], axis=0).T
        store_slabs(send.at[a], main0, main1, third)

    lane = lax.broadcasted_iota(jnp.int32, (1, 256), 1)

    @pl.loop(0, GROUPS)
    def _(g):
        for a in range(4):
            t_wait(a, g)

        @pl.when(g == GROUPS - 1)
        def _():
            s_start(0, 0)
            s_start(1, 0)

        carry = None
        for p in range(SPACE):
            window = slice(128 * p, 128 * p + 256)
            first = 16 * p
            m0 = jnp.where((lane >= first) & (lane < first + E), 1.0, 0.0).astype(BF16)
            m1 = jnp.where((lane >= first + E) & (lane < first + 2 * E), 1.0, 0.0).astype(BF16)

            def stacked(x):
                return jnp.concatenate([x * m0, x * m1], axis=0)

            q, k, c, v = (
                tin[a, :, g, :, window].astype(F32).reshape(ROWS, 256).astype(BF16) for a in range(4)
            )
            k2 = stacked(k)
            scores = dot(q, k2, NT)
            dprob = dot(c, stacked(v), NT)
            ds, low_t, ds_t = [], [], []
            for n in range(2):
                part = slice(128 * n, 128 * n + 128)
                pr = softmax(scores[:, part] * (SCALE * LOG2E) + bias[2 * p + n])
                low = pr.astype(BF16)
                d = score_grads(pr, low, dprob[:, part])
                ds.append(d)
                low_t.append(low.astype(F32).T.astype(BF16))
                ds_t.append(d.astype(F32).T.astype(BF16))
            outs = (
                dot(jnp.concatenate(ds, axis=1), k2) * SCALE,
                dot(jnp.concatenate(ds_t, axis=1), stacked(q)) * SCALE,
                dot(jnp.concatenate(low_t, axis=1), stacked(c)),
            )
            for n, out in enumerate(outs):
                left = out[:, :128] if carry is None else out[:, :128] + carry[n]
                joined[:, D * n + 128 * p:D * n + 128 * p + 128] = left.astype(BF16)
                if p == SPACE - 1:
                    joined[:, D * n + 1024:D * n + D] = out[:, 128:].astype(BF16)
            carry = [out[:, 128:] for out in outs]
        tin[0, :, g] = dot(joined[...], wq[...], NT).reshape(FRAMES, 8, D).astype(BF16)
        g_start(g)

    s_start(2, 0)
    for g in range(GROUPS):
        g_wait(g)
    gm_out = pltpu.make_async_copy(gm_in, gm, local_sem.at[6])
    gm_out.start()
    mid = gm_in[...].astype(F32).reshape(CLIPS, TOKENS, D)
    mid = jnp.concatenate([mid[0, :128], mid[1, :128], mid[0, 128:], mid[1, 128:]], axis=0).astype(BF16)
    cot_t = dot(wo[...], mid, NT)
    store_slabs(send.at[3], cot_t[:, :128], cot_t[:, 128:256], cot_t[:, 256:])
    s_start(3, 0)
    for a in range(4):
        s_start(a, 1)

    def gather(a, clip, head, dst):
        for s in range(SPACE):
            dst[:, 128 * s:128 * s + 128] = recv[a, s, clip, head]
        for m in range(SPACE // 2):
            low = recv[a, 2 * m, clip, 2].astype(F32)
            high = recv[a, 2 * m + 1, clip, 2].astype(F32)
            if head == 0:
                high = pltpu.roll(high, 64, 1)
            else:
                low = pltpu.roll(low, 64, 1)
            dst[:, 1024 + 128 * m:1152 + 128 * m] = halves(low, high).astype(BF16)

    def scatter(a, clip, head, tile, value):
        if tile < SPACE:
            send[a, tile, clip, head] = value.astype(BF16)
        elif head == 0:
            thirds[a, tile - SPACE] = value
        else:
            m = tile - SPACE
            other = thirds[a, m]
            send[a, 2 * m, clip, 2] = halves(other, pltpu.roll(value, 64, 1)).astype(BF16)
            send[a, 2 * m + 1, clip, 2] = halves(pltpu.roll(other, 64, 1), value).astype(BF16)

    @pl.loop(0, CLIPS)
    def _(clip):
        s_wait(0, clip)
        s_wait(1, clip)
        for head in range(2):
            gather(0, clip, head, q_t.at[head])
            gather(1, clip, head, k_t.at[head])
            row_n[...] = q_t[head].astype(F32).T.astype(BF16)
            for b in range(SEQ // BLOCK):
                block = slice(b * BLOCK, (b + 1) * BLOCK)
                scores = dot(row_n[block], k_t[head]) * (SCALE * LOG2E)
                probs[head, block] = softmax(scores).astype(BF16)
        s_wait(2, clip)
        s_wait(3, clip)
        for head in range(2):
            gather(2, clip, head, v_t)
            gather(3, clip, head, c_t)
            row_n[...] = c_t[...].astype(F32).T.astype(BF16)
            for b in range(SEQ // BLOCK):
                block = slice(b * BLOCK, (b + 1) * BLOCK)
                low = probs[head, block]
                ds = score_grads(low.astype(F32), low, dot(row_n[block], v_t[...]))
                to_q = dot(k_t[head], ds, NT) * SCALE
                for n in range(BLOCK // 128):
                    tile = b * (BLOCK // 128) + n
                    scatter(0, clip, head, tile, to_q[:, 128 * n:128 * n + 128])
                    if tile < SPACE:
                        b_start(0, tile, clip, head)
                to_k = dot(q_t[head, :, block], ds)
                to_v = dot(c_t[:, block], low)
                if b > 0:
                    to_k, to_v = sum_k[...] + to_k, sum_v[...] + to_v
                if b < SEQ // BLOCK - 1:
                    sum_k[...], sum_v[...] = to_k, to_v
            to_k = to_k * SCALE
            for n in range(SEQ // 128):
                scatter(1, clip, head, n, to_k[:, 128 * n:128 * n + 128])
                scatter(2, clip, head, n, to_v[:, 128 * n:128 * n + 128])
            b_start_all(1, clip, head)
            b_start_all(2, clip, head)
            if head == 1:
                for a in range(3):
                    b_start_all(a, clip, 2)

    outs = []
    for clip in range(CLIPS):
        own = [
            pltpu.make_async_copy(send.at[a, ms, clip], back.at[a, ms, clip], local_sem.at[a])
            for a in range(3)
        ]
        for copy in own:
            copy.start()
        for a, out in enumerate((gq, gk, gv)):
            own[a].wait()
            b_wait(a, clip)
            main = back[a, :, clip, 0:2].astype(F32).reshape(D, 128)
            sin[a, clip, 0:128, :] = main.T.astype(BF16)
            third = back[a, :, clip, 2].astype(F32)
            odd = pltpu.roll(third.reshape(SPACE * E, 128), 64, 1).reshape(SPACE, 1, E, 128)
            third = jnp.concatenate([third.reshape(SPACE, 1, E, 128), odd], axis=1).reshape(D, 128)
            sin[a, clip, 128:192, :] = third.T[0:64].astype(BF16)
            outs.append(pltpu.make_async_copy(sin.at[a, clip], out.at[clip], out_sem.at[a, clip]))
            outs[-1].start()
    gm_out.wait()
    for copy in outs:
        copy.wait()


def copy_kernel(a, b, c, d, a_out, b_out, c_out, d_out, held, in_sem, out_sem):
    pairs = ((a, a_out), (b, b_out), (c, c_out), (d, d_out))
    reads = [pltpu.make_async_copy(src, held.at[n], in_sem.at[n]) for n, (src, _) in enumerate(pairs)]
    writes = [pltpu.make_async_copy(held.at[n], dst, out_sem.at[n]) for n, (_, dst) in enumerate(pairs)]
    for copy in reads:
        copy.start()
    for read, write in zip(reads, writes):
        read.wait()
        write.start()
    for copy in writes:
        copy.wait()


def on_device(
    q_spatial, k_spatial, v_spatial, q_temporal, k_temporal, v_temporal, grad_out,
    inpaint_mask, frame_order, rel_bias, w_qkv, w_out,
):
    chunks = (FRAMES, GROUPS, 8, D)
    shape = (CLIPS, TOKENS, D)
    slabs = (SPACE, CLIPS, 3, E, 128)
    hbm = pl.BlockSpec(memory_space=pl.ANY)
    vmem = pl.BlockSpec(memory_space=pltpu.VMEM)
    smem = pl.BlockSpec(memory_space=pltpu.SMEM)
    dma = pltpu.SemaphoreType.DMA
    results = pl.pallas_call(
        kernel,
        out_shape=(jax.ShapeDtypeStruct(shape, BF16),) * 3 + (jax.ShapeDtypeStruct(chunks, BF16),),
        in_specs=[hbm, hbm, hbm, hbm, vmem, smem, smem, hbm, hbm, hbm, hbm, hbm],
        out_specs=(hbm,) * 4,
        scratch_shapes=[
            pltpu.VMEM(chunks, BF16),
            pltpu.VMEM((4,) + chunks, BF16),
            pltpu.VMEM((HEADS, ROWS, ROWS), F32),
            pltpu.VMEM((ROWS, 3 * D), BF16),
            pltpu.VMEM(chunks, BF16),
            pltpu.VMEM((3,) + shape, BF16),
            pltpu.VMEM((4,) + slabs, BF16),
            pltpu.VMEM((4,) + slabs, BF16),
            pltpu.VMEM((3,) + slabs, BF16),
            pltpu.VMEM((D, 3 * D), BF16),
            pltpu.VMEM((D, D), BF16),
            pltpu.VMEM((2, SEQ, SEQ), BF16),
            *(pltpu.VMEM((2, E, SEQ), BF16) for _ in range(2)),
            *(pltpu.VMEM((E, SEQ), BF16) for _ in range(2)),
            pltpu.VMEM((SEQ, E), BF16),
            *(pltpu.VMEM((E, SEQ), F32) for _ in range(2)),
            pltpu.VMEM((3, 4, E, 128), F32),
            dma((4, GROUPS)), dma((4, GROUPS)), dma((GROUPS,)), dma((GROUPS,)),
            dma((4, CLIPS)), dma((4, CLIPS)), dma((3, CLIPS)), dma((3, CLIPS)),
            dma((7,)), dma((9, GROUPS)), dma((3, CLIPS)),
        ],
        compiler_params=pltpu.CompilerParams(
            collective_id=0, has_side_effects=True, vmem_limit_bytes=63 * 2**20
        ),
    )(
        q_temporal.reshape(chunks), k_temporal.reshape(chunks), v_temporal.reshape(chunks),
        grad_out.reshape(chunks), inpaint_mask, frame_order, rel_bias,
        q_spatial.reshape(shape), k_spatial.reshape(shape), v_spatial.reshape(shape), w_qkv, w_out,
    )
    flat = (CLIPS * TOKENS, D)
    results = pl.pallas_call(
        copy_kernel,
        out_shape=(jax.ShapeDtypeStruct(flat, BF16),) * 4,
        in_specs=[hbm] * 4,
        out_specs=(hbm,) * 4,
        scratch_shapes=[pltpu.VMEM((4,) + flat, BF16), dma((4,)), dma((4,))],
    )(*(r.reshape(flat) for r in results))
    return tuple(r.reshape(CLIPS, 1, TOKENS, D) for r in results)


def solution(mesh):
    split = P(None, "frame", "space", None)
    in_specs = (split,) * 7 + (P(None, "frame", "space"), P(), P(), P(), P())
    return jax.shard_map(
        on_device, mesh=mesh, in_specs=in_specs, out_specs=(split,) * 4, check_vma=False
    )
```

time: 149 us -> 139 us (0.933)
  Pallas kernels: 148 us -> 137 us
    pallas_call x1, Pallas kernels: 145 us -> 134 us  [on_device(): pl.pallas_call(kernel, out_shape=(jax.ShapeDtypeStruct(shape, BF16),) * 3...]
where the time goes in v3:
time: 139 us; the launch traced here: 138 us
  Pallas kernels  137 us (99%)
    pallas_call x1, Pallas kernels, on_device(): pl.pallas_call(kernel, out_shape=(jax.ShapeDtypeStruct(shape, BF16),) * 3...  134 us
    pallas_call x1, Pallas kernels, on_device(): pl.pallas_call(copy_kernel, out_shape=(jax.ShapeDtypeStruct(flat, BF16),)...  3.02 us

profile of v3, /device:TPU:0, one launch (start us, length us, event | category | flops | bytes accessed | tf_op | source)
XLA Modules:
  0.0 137.8 jit_solution(2025831748876740852)
XLA Ops:
  0.6 133.9 %shard_map.147 = (bf16[2,192,1152]{2,1,0:T(8,128)(2,1)}, bf16[2,192,1152]{2,1,0:T(8,128)(2,1)}, bf16[2,192,1152]{2,1,0:T(8,128)(2,1)}, bf16[16,3,8,1152]{3,2,1,0:T(8,128)(2,1)}) custom-call(bf16[16,3,8,1152]{3,2,1,0:T(8,128)(2,1)} %bitcast.27, bf16[16,3,8,1152]{3,2,1,0:T(8,128)(2,1)} %bitcast.28, bf16[16,3,8,1152]{3,2,1,0:T(8,128)(2,1)} %bitcast.29, ...), custom_call_target="tpu_custom_call" | custom-call | tf_op jit(solution)/shard_map/pallas_call | solution.py:387
  134.6 3.0 %shard_map.148 = (bf16[384,1152]{1,0:T(8,128)(2,1)}, bf16[384,1152]{1,0:T(8,128)(2,1)}, bf16[384,1152]{1,0:T(8,128)(2,1)}, bf16[384,1152]{1,0:T(8,128)(2,1)}) custom-call(bf16[384,1152]{1,0:T(8,128)(2,1)} %bitcast.23, bf16[384,1152]{1,0:T(8,128)(2,1)} %bitcast.24, bf16[384,1152]{1,0:T(8,128)(2,1)} %bitcast.25, bf16[384,1152]{1,0:T(8,128)(2,1)} %bitcast.26), custom_call_target="tpu_custom_call" | custom-call | tf_op jit(solution)/shard_map/pallas_call | solution.py:423

commit v4 on v3

--- a/solution.py
+++ b/solution.py
@@ -57,9 +57,9 @@
 
 
 def kernel(
-    qt, kt, vt, go, mask, order, rel_bias, qs, ks, vs, wqkv, wout,
+    qt, kt, vt, go, mask_in, order_in, bias_in, qs, ks, vs, wqkv, wout,
     gq, gk, gv, gm,
-    cot, tin, bias, joined, gm_in, sin, send, recv, back, wq, wo,
+    mask, order, rel_bias, cot, tin, bias, joined, gm_in, sin, send, recv, back, wq, wo,
     probs, q_t, k_t, v_t, c_t, row_n, sum_k, sum_v, thirds,
     t_send_sem, t_recv_sem, g_send_sem, g_recv_sem, s_send_sem, s_recv_sem, b_send_sem, b_recv_sem,
     local_sem, own_sem, out_sem,
@@ -78,10 +78,14 @@
     loads = [
         pltpu.make_async_copy(src, dst, local_sem.at[n])
         for n, (src, dst) in enumerate(
-            ((go, cot), (qs, sin.at[0]), (ks, sin.at[1]), (vs, sin.at[2]), (wqkv, wq), (wout, wo))
+            (
+                (go, cot), (mask_in, mask), (order_in, order), (bias_in, rel_bias),
+                (qs, sin.at[0]), (ks, sin.at[1]), (vs, sin.at[2]), (wqkv, wq), (wout, wo),
+            )
         )
     ]
-    loads[0].start()
+    for copy in loads[:4]:
+        copy.start()
     pl.semaphore_wait(barrier, FRAMES + SPACE - 2)
 
     sources = (qt, kt, cot, vt)
@@ -140,33 +144,37 @@
             pltpu.make_async_copy(some, some, sem).wait()
 
     def b_start(a, peer, clip, slab):
+        kind = slab // 2
+
         @pl.when(peer != ms)
         def _():
             pltpu.make_async_remote_copy(
                 src_ref=send.at[a, peer, clip, slab], dst_ref=back.at[a, ms, clip, slab],
-                send_sem=b_send_sem.at[a, clip], recv_sem=b_recv_sem.at[a, clip],
+                send_sem=b_send_sem.at[a, clip, kind], recv_sem=b_recv_sem.at[a, clip, kind],
                 device_id=(mf, peer), device_id_type=MESH,
             ).start()
 
     def b_start_all(a, clip, slab):
+        kind = slab // 2
         for i in (1, 7, 3, 5, 2, 4, 6):
             peer = lax.rem(ms + i, SPACE)
             pltpu.make_async_remote_copy(
                 src_ref=send.at[a, peer, clip, slab], dst_ref=back.at[a, ms, clip, slab],
-                send_sem=b_send_sem.at[a, clip], recv_sem=b_recv_sem.at[a, clip],
+                send_sem=b_send_sem.at[a, clip, kind], recv_sem=b_recv_sem.at[a, clip, kind],
                 device_id=(mf, peer), device_id_type=MESH,
             ).start()
 
-    def b_wait(a, clip):
-        some = back.at[a, 0:SPACE - 1, clip]
-        sems = (b_send_sem.at[a, clip], b_recv_sem.at[a, clip])
+    def b_wait(a, clip, kind):
+        some = back.at[a, 0:SPACE - 1, clip, 2 * kind:2 + kind]
+        sems = (b_send_sem.at[a, clip, kind], b_recv_sem.at[a, clip, kind])
         for sem in sems:
             pltpu.make_async_copy(some, some, sem).wait()
 
     t_start(0, 0)
     t_start(1, 0)
     t_start(3, 0)
-    loads[0].wait()
+    for copy in loads[:4]:
+        copy.wait()
     row = lax.broadcasted_iota(jnp.int32, (TOKENS, TOKENS), 0)
     col = lax.broadcasted_iota(jnp.int32, (TOKENS, TOKENS), 1)
     for clip in range(CLIPS):
@@ -177,7 +185,7 @@
     for g in range(1, GROUPS):
         for a in range(4):
             t_start(a, g)
-    for copy in loads[1:]:
+    for copy in loads[4:]:
         copy.start()
 
     row = lax.broadcasted_iota(jnp.int32, (ROWS, ROWS), 0)
@@ -194,7 +202,7 @@
             total = jnp.where(offset == o, rel_bias[h, o] * LOG2E, total)
         bias[h] = total
 
-    for copy in loads[1:]:
+    for copy in loads[4:]:
         copy.wait()
 
     @pl.loop(0, 3)
@@ -257,17 +265,19 @@
         g_start(g)
 
     s_start(2, 0)
+    s_start(0, 1)
+    s_start(1, 1)
     for g in range(GROUPS):
         g_wait(g)
-    gm_out = pltpu.make_async_copy(gm_in, gm, local_sem.at[6])
+    gm_out = pltpu.make_async_copy(gm_in, gm, local_sem.at[9])
     gm_out.start()
     mid = gm_in[...].astype(F32).reshape(CLIPS, TOKENS, D)
     mid = jnp.concatenate([mid[0, :128], mid[1, :128], mid[0, 128:], mid[1, 128:]], axis=0).astype(BF16)
     cot_t = dot(wo[...], mid, NT)
     store_slabs(send.at[3], cot_t[:, :128], cot_t[:, 128:256], cot_t[:, 256:])
     s_start(3, 0)
-    for a in range(4):
-        s_start(a, 1)
+    s_start(2, 1)
+    s_start(3, 1)
 
     def gather(a, clip, head, dst):
         for s in range(SPACE):
@@ -344,11 +354,14 @@
         ]
         for copy in own:
             copy.start()
-        for a, out in enumerate((gq, gk, gv)):
-            own[a].wait()
-            b_wait(a, clip)
+        for copy in own:
+            copy.wait()
+        for a in range(3):
+            b_wait(a, clip, 0)
             main = back[a, :, clip, 0:2].astype(F32).reshape(D, 128)
             sin[a, clip, 0:128, :] = main.T.astype(BF16)
+        for a, out in enumerate((gq, gk, gv)):
+            b_wait(a, clip, 1)
             third = back[a, :, clip, 2].astype(F32)
             odd = pltpu.roll(third.reshape(SPACE * E, 128), 64, 1).reshape(SPACE, 1, E, 128)
             third = jnp.concatenate([third.reshape(SPACE, 1, E, 128), odd], axis=1).reshape(D, 128)
@@ -361,9 +374,12 @@
 
 
 def copy_kernel(a, b, c, d, a_out, b_out, c_out, d_out, held, in_sem, out_sem):
-    pairs = ((a, a_out), (b, b_out), (c, c_out), (d, d_out))
-    reads = [pltpu.make_async_copy(src, held.at[n], in_sem.at[n]) for n, (src, _) in enumerate(pairs)]
-    writes = [pltpu.make_async_copy(held.at[n], dst, out_sem.at[n]) for n, (_, dst) in enumerate(pairs)]
+    reads, writes = [], []
+    for n, (src, dst) in enumerate(((a, a_out), (b, b_out), (c, c_out), (d, d_out))):
+        for half in range(2):
+            rows = slice(192 * half, 192 * half + 192)
+            reads.append(pltpu.make_async_copy(src.at[rows], held.at[n, rows], in_sem.at[n, half]))
+            writes.append(pltpu.make_async_copy(held.at[n, rows], dst.at[rows], out_sem.at[n, half]))
     for copy in reads:
         copy.start()
     for read, write in zip(reads, writes):
@@ -381,15 +397,16 @@
     shape = (CLIPS, TOKENS, D)
     slabs = (SPACE, CLIPS, 3, E, 128)
     hbm = pl.BlockSpec(memory_space=pl.ANY)
-    vmem = pl.BlockSpec(memory_space=pltpu.VMEM)
-    smem = pl.BlockSpec(memory_space=pltpu.SMEM)
     dma = pltpu.SemaphoreType.DMA
     results = pl.pallas_call(
         kernel,
         out_shape=(jax.ShapeDtypeStruct(shape, BF16),) * 3 + (jax.ShapeDtypeStruct(chunks, BF16),),
-        in_specs=[hbm, hbm, hbm, hbm, vmem, smem, smem, hbm, hbm, hbm, hbm, hbm],
+        in_specs=[hbm] * 12,
         out_specs=(hbm,) * 4,
         scratch_shapes=[
+            pltpu.VMEM((CLIPS, 1, TOKENS), jnp.int32),
+            pltpu.SMEM((FRAMES,), jnp.int32),
+            pltpu.SMEM((HEADS, 2 * FRAMES - 1), F32),
             pltpu.VMEM(chunks, BF16),
             pltpu.VMEM((4,) + chunks, BF16),
             pltpu.VMEM((HEADS, ROWS, ROWS), F32),
@@ -408,8 +425,8 @@
             *(pltpu.VMEM((E, SEQ), F32) for _ in range(2)),
             pltpu.VMEM((3, 4, E, 128), F32),
             dma((4, GROUPS)), dma((4, GROUPS)), dma((GROUPS,)), dma((GROUPS,)),
-            dma((4, CLIPS)), dma((4, CLIPS)), dma((3, CLIPS)), dma((3, CLIPS)),
-            dma((7,)), dma((9, GROUPS)), dma((3, CLIPS)),
+            dma((4, CLIPS)), dma((4, CLIPS)), dma((3, CLIPS, 2)), dma((3, CLIPS, 2)),
+            dma((10,)), dma((9, GROUPS)), dma((3, CLIPS)),
         ],
         compiler_params=pltpu.CompilerParams(
             collective_id=0, has_side_effects=True, vmem_limit_bytes=63 * 2**20
@@ -425,7 +442,7 @@
         out_shape=(jax.ShapeDtypeStruct(flat, BF16),) * 4,
         in_specs=[hbm] * 4,
         out_specs=(hbm,) * 4,
-        scratch_shapes=[pltpu.VMEM((4,) + flat, BF16), dma((4,)), dma((4,))],
+        scratch_shapes=[pltpu.VMEM((4,) + flat, BF16), dma((4, 2)), dma((4, 2))],
     )(*(r.reshape(flat) for r in results))
     return tuple(r.reshape(CLIPS, 1, TOKENS, D) for r in results)
 

time: 139 us -> 137 us (0.986); the launches traced: 138 us -> 137 us
  no operation moved by 1% of the time
where the time goes in v4:
time: 137 us
  Pallas kernels  137 us (100%)
    pallas_call x1, Pallas kernels, on_device(): pl.pallas_call(kernel, out_shape=(jax.ShapeDtypeStruct(shape, BF16),) * 3...  134 us
    pallas_call x1, Pallas kernels, on_device(): pl.pallas_call(copy_kernel, out_shape=(jax.ShapeDtypeStruct(flat, BF16),)...  2.94 us

profile of v4, /device:TPU:0, one launch (start us, length us, event | category | flops | bytes accessed | tf_op | source)
XLA Modules:
  0.0 137.4 jit_solution(5425022475248356612)
XLA Ops:
  0.6 133.6 %shard_map.147 = (bf16[2,192,1152]{2,1,0:T(8,128)(2,1)}, bf16[2,192,1152]{2,1,0:T(8,128)(2,1)}, bf16[2,192,1152]{2,1,0:T(8,128)(2,1)}, bf16[16,3,8,1152]{3,2,1,0:T(8,128)(2,1)}) custom-call(bf16[16,3,8,1152]{3,2,1,0:T(8,128)(2,1)} %bitcast.27, bf16[16,3,8,1152]{3,2,1,0:T(8,128)(2,1)} %bitcast.28, bf16[16,3,8,1152]{3,2,1,0:T(8,128)(2,1)} %bitcast.29, ...), custom_call_target="tpu_custom_call" | custom-call | tf_op jit(solution)/shard_map/pallas_call | solution.py:401
  134.3 2.9 %shard_map.148 = (bf16[384,1152]{1,0:T(8,128)(2,1)}, bf16[384,1152]{1,0:T(8,128)(2,1)}, bf16[384,1152]{1,0:T(8,128)(2,1)}, bf16[384,1152]{1,0:T(8,128)(2,1)}) custom-call(bf16[384,1152]{1,0:T(8,128)(2,1)} %bitcast.23, bf16[384,1152]{1,0:T(8,128)(2,1)} %bitcast.24, bf16[384,1152]{1,0:T(8,128)(2,1)} %bitcast.25, bf16[384,1152]{1,0:T(8,128)(2,1)} %bitcast.26), custom_call_target="tpu_custom_call" | custom-call | tf_op jit(solution)/shard_map/pallas_call | solution.py:440

commit v5 on v4

--- a/solution.py
+++ b/solution.py
@@ -19,6 +19,7 @@
 SCALE = E ** (-0.5)
 LOG2E = 1.4426950408889634
 MESH = pl.DeviceIdType.MESH
+FRAME_ORDER = (12, 2, 10, 14, 6, 4, 8, 11, 3, 13, 5, 9, 7, 15, 1)
 NN = (((1,), (0,)), ((), ()))
 NT = (((1,), (1,)), ((), ()))
 F32 = jnp.float32
@@ -91,8 +92,7 @@
     sources = (qt, kt, cot, vt)
 
     def t_start(a, g):
-        @pl.loop(1, FRAMES)
-        def _(i):
+        for i in FRAME_ORDER:
             peer = lax.rem(mf + i, FRAMES)
             pltpu.make_async_remote_copy(
                 src_ref=sources[a].at[peer, g], dst_ref=tin.at[a, mf, g],

time: 137 us -> 134 us (0.978); the launches traced: 137 us -> 132 us
  Pallas kernels: 137 us -> 131 us
    pallas_call x1, Pallas kernels: 134 us -> 128 us  [on_device(): pl.pallas_call(kernel, out_shape=(jax.ShapeDtypeStruct(shape, BF16),) * 3...]
where the time goes in v5:
time: 134 us; the launch traced here: 132 us
  Pallas kernels  131 us (98%)
    pallas_call x1, Pallas kernels, on_device(): pl.pallas_call(kernel, out_shape=(jax.ShapeDtypeStruct(shape, BF16),) * 3...  128 us
    pallas_call x1, Pallas kernels, on_device(): pl.pallas_call(copy_kernel, out_shape=(jax.ShapeDtypeStruct(flat, BF16),)...  2.94 us

profile of v5, /device:TPU:0, one launch (start us, length us, event | category | flops | bytes accessed | tf_op | source)
XLA Modules:
  0.0 132.2 jit_solution(10215622870187369018)
XLA Ops:
  0.6 128.5 %shard_map.147 = (bf16[2,192,1152]{2,1,0:T(8,128)(2,1)}, bf16[2,192,1152]{2,1,0:T(8,128)(2,1)}, bf16[2,192,1152]{2,1,0:T(8,128)(2,1)}, bf16[16,3,8,1152]{3,2,1,0:T(8,128)(2,1)}) custom-call(bf16[16,3,8,1152]{3,2,1,0:T(8,128)(2,1)} %bitcast.27, bf16[16,3,8,1152]{3,2,1,0:T(8,128)(2,1)} %bitcast.28, bf16[16,3,8,1152]{3,2,1,0:T(8,128)(2,1)} %bitcast.29, ...), custom_call_target="tpu_custom_call" | custom-call | tf_op jit(solution)/shard_map/pallas_call | solution.py:401
  129.1 2.9 %shard_map.148 = (bf16[384,1152]{1,0:T(8,128)(2,1)}, bf16[384,1152]{1,0:T(8,128)(2,1)}, bf16[384,1152]{1,0:T(8,128)(2,1)}, bf16[384,1152]{1,0:T(8,128)(2,1)}) custom-call(bf16[384,1152]{1,0:T(8,128)(2,1)} %bitcast.23, bf16[384,1152]{1,0:T(8,128)(2,1)} %bitcast.24, bf16[384,1152]{1,0:T(8,128)(2,1)} %bitcast.25, bf16[384,1152]{1,0:T(8,128)(2,1)} %bitcast.26), custom_call_target="tpu_custom_call" | custom-call | tf_op jit(solution)/shard_map/pallas_call | solution.py:440
